TPU v7x, 32 devices: a whole 2x2x4 slice. The times are simulated.
32 devices in a mesh: dp: 4 (over z), fsdp: 8 (over y, x, core).
Axes of the slice: x: 2, y: 2, z: 4, core: 2. Of those that a mesh axis runs over, the one named last changes fastest.
Arguments:
- windows: float32 [27648, 3600], P(('dp', 'fsdp')), may hold values from -6 to 6
- targets: float32 [27648, 720], P(('dp', 'fsdp')), may hold values from -24 to 24
- horizon: int32 [27648], P(('dp', 'fsdp')), may hold values from 96 to 720, as said below
- step_count: int32 [1], replicated, may hold values from 2 to 20
- first_w: float32 [4950, 512], P(None, 'fsdp'), may hold values from -0.1875 to 0.1875
- first_w_avg: float32 [4950, 512], P(None, 'fsdp'), may hold values from -5.722046e-06 to 5.722046e-06
- first_w_sq: float32 [4950, 512], P(None, 'fsdp'), may hold values from 1.1100048e-14 to 4.4400193e-14
- hidden_w: float32 [3, 3, 512, 512], P(None, None, 'fsdp'), may hold values from -0.375 to 0.375
- hidden_w_avg: float32 [3, 3, 512, 512], P(None, None, 'fsdp'), may hold values from -5.722046e-06 to 5.722046e-06
- hidden_w_sq: float32 [3, 3, 512, 512], P(None, None, 'fsdp'), may hold values from 1.1100048e-14 to 4.4400193e-14
- back_w: float32 [2, 512, 3600], P(None, 'fsdp'), may hold values from -0.375 to 0.375
- back_w_avg: float32 [2, 512, 3600], P(None, 'fsdp'), may hold values from -5.722046e-06 to 5.722046e-06
- back_w_sq: float32 [2, 512, 3600], P(None, 'fsdp'), may hold values from 1.1100048e-14 to 4.4400193e-14
- fore_w: float32 [512, 810], P('fsdp'), may hold values from -0.09375 to 0.09375
- fore_w_avg: float32 [512, 810], P('fsdp'), may hold values from -5.722046e-06 to 5.722046e-06
- fore_w_sq: float32 [512, 810], P('fsdp'), may hold values from 1.1100048e-14 to 4.4400193e-14
- bias_vec: float32 [14154], replicated, may hold values from -1.5 to 1.5
- bias_avg: float32 [14154], replicated, may hold values from -2.2888184e-05 to 2.2888184e-05
- bias_sq: float32 [14154], replicated, may hold values from 1.7760077e-13 to 7.104031e-13
Outputs:
- loss: float32 [], replicated
- grad_norm: float32 [], replicated
- new_first_avg: float32 [4950, 512], P(None, 'fsdp')
- new_first_sq: float32 [4950, 512], P(None, 'fsdp')
- new_first_w: float32 [4950, 512], P(None, 'fsdp')
- new_hidden_avg: float32 [3, 3, 512, 512], P(None, None, 'fsdp')
- new_hidden_sq: float32 [3, 3, 512, 512], P(None, None, 'fsdp')
- new_hidden_w: float32 [3, 3, 512, 512], P(None, None, 'fsdp')
- new_back_avg: float32 [2, 512, 3600], P(None, 'fsdp')
- new_back_sq: float32 [2, 512, 3600], P(None, 'fsdp')
- new_back_w: float32 [2, 512, 3600], P(None, 'fsdp')
- new_fore_avg: float32 [512, 810], P('fsdp')
- new_fore_sq: float32 [512, 810], P('fsdp')
- new_fore_w: float32 [512, 810], P('fsdp')
- new_bias_avg: float32 [14154], replicated
- new_bias_sq: float32 [14154], replicated
- new_bias_vec: float32 [14154], replicated
- first_copy: bfloat16 [4950, 512], P(None, 'fsdp')
- hidden_copy: bfloat16 [3, 3, 512, 512], P(None, None, 'fsdp')
- back_copy: bfloat16 [2, 512, 3600], P(None, 'fsdp')
- fore_copy: bfloat16 [512, 810], P('fsdp')
Inputs may be any that keep to these rules, and one draw needn't show every extreme that they name: Each horizon is 96, 336 or 720.
All inputs are finite; a program needn't handle non-finite values.
Results may differ from a plain program's by a relative error of at most 0.006.
Values may be sent and summed in bfloat16 or wider, within the bound.
A program may use at most 256 MiB of HBM per device.

v0:
```python
import jax
import jax.numpy as jnp
import numpy as np
from jax import lax
from jax.sharding import PartitionSpec as P

KERNELS = (8, 4, 1)
RATIOS = (24, 12, 1)
CLIP_MAX = 0.01
RATE = 0.02
BETA_ONE = 0.9
BETA_TWO = 0.999
EPSILON = 1e-08
DECAY = 0.01
DOT_EXACTNESS = lax.Precision.HIGHEST


def blend_coefficients(fine, coarse):
    column = np.arange(fine)
    numer = np.maximum((2 * column + 1) * coarse - fine, 0)
    lower_idx = numer // (2 * fine)
    frac = (numer - lower_idx * 2 * fine) / (2.0 * fine)
    upper_idx = np.minimum(lower_idx + 1, coarse - 1)
    matrix = np.zeros((coarse, fine), np.float32)
    matrix[lower_idx, column] += 1.0 - frac
    matrix[upper_idx, column] += frac
    return matrix


def normalize(windows, targets):
    center = jnp.mean(windows, axis=1, keepdims=True)
    spread = jnp.sqrt(jnp.mean((windows - center) ** 2, axis=1, keepdims=True) + 1e-05)
    return ((windows - center) / spread, (targets - center) / spread)


def mean_pool(values, kernel):
    if kernel == 1:
        return values
    return jnp.mean(values.reshape(values.shape[0], values.shape[1] // kernel, kernel), axis=2)


def pool_back(d_pooled, kernel):
    if kernel == 1:
        return d_pooled
    spread_out = jnp.broadcast_to((d_pooled / kernel)[:, :, None], d_pooled.shape + (kernel,))
    return spread_out.reshape(d_pooled.shape[0], d_pooled.shape[1] * kernel)


def silu_slope(pre_act):
    gate = jax.nn.sigmoid(pre_act)
    return gate * (1.0 + pre_act * (1.0 - gate))


def stack_params(stack_id, gathered, bias_vec, length, steps_ahead_total):
    first_full, hidden_full, back_full, fore_full = gathered
    hidden_size = hidden_full.shape[-1]
    row_start = sum((length // KERNELS[earlier] for earlier in range(stack_id)))
    col_start = sum((steps_ahead_total // RATIOS[earlier] for earlier in range(stack_id)))
    pooled_len = length // KERNELS[stack_id]
    anchor_entries = steps_ahead_total // RATIOS[stack_id]
    layers = [
        (
            first_full[row_start : row_start + pooled_len],
            bias_vec[stack_id * hidden_size : (stack_id + 1) * hidden_size],
        )
    ]
    for layer_id in range(3):
        offset = (3 + 3 * stack_id + layer_id) * hidden_size
        layers.append((hidden_full[stack_id, layer_id], bias_vec[offset : offset + hidden_size]))
    fore_start = 12 * hidden_size + 2 * length + col_start
    fore_pair = (
        fore_full[:, col_start : col_start + anchor_entries],
        bias_vec[fore_start : fore_start + anchor_entries],
    )
    back_pair = None
    if stack_id < 2:
        back_start = 12 * hidden_size + stack_id * length
        back_pair = (back_full[stack_id], bias_vec[back_start : back_start + length])
    linear_upsample_anchors = jnp.asarray(blend_coefficients(steps_ahead_total, anchor_entries))
    return (layers, fore_pair, back_pair, linear_upsample_anchors)


def stack_forward(residual, stack_id, layers, fore_pair, back_pair, linear_upsample_anchors):
    inputs_kept = [mean_pool(residual, KERNELS[stack_id]).astype(jnp.bfloat16)]
    pre_kept = []
    for weight, bias in layers:
        pre_act = jnp.dot(inputs_kept[-1], weight, preferred_element_type=jnp.float32) + bias
        pre_kept.append(pre_act)
        inputs_kept.append(jax.nn.silu(pre_act).astype(jnp.bfloat16))
    anchor_result = (
        jnp.dot(inputs_kept[-1], fore_pair[0], preferred_element_type=jnp.float32) + fore_pair[1]
    )
    running_subtotal = jnp.dot(anchor_result, linear_upsample_anchors, precision=DOT_EXACTNESS)
    backcast = None
    if back_pair is not None:
        backcast = (
            jnp.dot(inputs_kept[-1], back_pair[0], preferred_element_type=jnp.float32)
            + back_pair[1]
        )
    return ((inputs_kept, pre_kept), running_subtotal, backcast)


def head_grads(last_act, d_low, weight):
    grad_w = jnp.dot(last_act.T, d_low, preferred_element_type=jnp.float32)
    grad_b = jnp.sum(d_low.astype(jnp.float32), axis=0)
    return ((grad_w, grad_b), jnp.dot(d_low, weight.T, preferred_element_type=jnp.float32))


def stack_backward(kept, anchor_cotangent, d_backcast, layers, fore_pair, back_pair, need_input):
    inputs_kept, pre_kept = kept
    last_act = inputs_kept[-1]
    fore_grads, d_hidden = head_grads(last_act, anchor_cotangent.astype(jnp.bfloat16), fore_pair[0])
    back_grads = None
    if back_pair is not None:
        back_grads, d_extra = head_grads(last_act, d_backcast.astype(jnp.bfloat16), back_pair[0])
        d_hidden = d_hidden + d_extra
    layer_grads = [None, None, None, None]
    for layer_id in (3, 2, 1, 0):
        d_pre = (d_hidden * silu_slope(pre_kept[layer_id])).astype(jnp.bfloat16)
        layer_grads[layer_id] = (
            jnp.dot(inputs_kept[layer_id].T, d_pre, preferred_element_type=jnp.float32),
            jnp.sum(d_pre.astype(jnp.float32), axis=0),
        )
        if layer_id > 0 or need_input:
            d_hidden = jnp.dot(d_pre, layers[layer_id][0].T, preferred_element_type=jnp.float32)
    return (layer_grads, fore_grads, back_grads, d_hidden)


def adamw(weight, avg, square, grad, step_float):
    new_avg = BETA_ONE * avg + (1.0 - BETA_ONE) * grad
    new_sq = BETA_TWO * square + (1.0 - BETA_TWO) * grad * grad
    avg_hat = new_avg / (1.0 - BETA_ONE**step_float)
    sq_hat = new_sq / (1.0 - BETA_TWO**step_float)
    new_weight = weight - RATE * (avg_hat / (jnp.sqrt(sq_hat) + EPSILON) + DECAY * weight)
    return (new_avg, new_sq, new_weight)


def body(
    windows,
    targets,
    horizon,
    step_count,
    first_w,
    first_w_avg,
    first_w_sq,
    hidden_w,
    hidden_w_avg,
    hidden_w_sq,
    back_w,
    back_w_avg,
    back_w_sq,
    fore_w,
    fore_w_avg,
    fore_w_sq,
    bias_vec,
    bias_avg,
    bias_sq,
):
    length = windows.shape[1]
    steps_ahead_total = targets.shape[1]
    normed, observed_future = normalize(windows, targets)
    future_usable_flags = (
        jnp.arange(steps_ahead_total, dtype=jnp.int32)[None, :] < horizon[:, None]
    ).astype(jnp.float32)
    usable_tally = lax.psum(jnp.sum(horizon.astype(jnp.float32)), ("dp", "fsdp"))
    shards = (
        first_w.astype(jnp.bfloat16),
        hidden_w.astype(jnp.bfloat16),
        back_w.astype(jnp.bfloat16),
        fore_w.astype(jnp.bfloat16),
    )
    gathered = (
        lax.all_gather(shards[0], "fsdp", axis=1, tiled=True),
        lax.all_gather(shards[1], "fsdp", axis=2, tiled=True),
        lax.all_gather(shards[2], "fsdp", axis=1, tiled=True),
        lax.all_gather(shards[3], "fsdp", axis=0, tiled=True),
    )
    residual = normed
    kept_stacks = []
    predicted_future = jnp.zeros(observed_future.shape, jnp.float32)
    for stack_id in range(3):
        layers, fore_pair, back_pair, linear_upsample_anchors = stack_params(
            stack_id, gathered, bias_vec, length, steps_ahead_total
        )
        kept, running_subtotal, backcast = stack_forward(
            residual, stack_id, layers, fore_pair, back_pair, linear_upsample_anchors
        )
        kept_stacks.append(kept)
        predicted_future = predicted_future + running_subtotal
        if backcast is not None:
            residual = residual - backcast
    residual_difference = predicted_future - observed_future
    loss_part = (
        jnp.sum(future_usable_flags * residual_difference * residual_difference) / usable_tally
    )
    future_slope_cotangent = 2.0 * future_usable_flags * residual_difference / usable_tally
    again = (
        lax.all_gather(shards[0], "fsdp", axis=1, tiled=True),
        lax.all_gather(shards[1], "fsdp", axis=2, tiled=True),
        lax.all_gather(shards[2], "fsdp", axis=1, tiled=True),
        lax.all_gather(shards[3], "fsdp", axis=0, tiled=True),
    )
    results = [None, None, None]
    d_residual = None
    for stack_id in (2, 1, 0):
        layers, fore_pair, back_pair, linear_upsample_anchors = stack_params(
            stack_id, again, bias_vec, length, steps_ahead_total
        )
        anchor_cotangent = jnp.dot(
            future_slope_cotangent, linear_upsample_anchors.T, precision=DOT_EXACTNESS
        )
        d_backcast = None if d_residual is None else -d_residual
        results[stack_id] = stack_backward(
            kept_stacks[stack_id],
            anchor_cotangent,
            d_backcast,
            layers,
            fore_pair,
            back_pair,
            stack_id > 0,
        )
        if stack_id > 0:
            spread_back = pool_back(results[stack_id][3], KERNELS[stack_id])
            d_residual = spread_back if d_residual is None else d_residual + spread_back
    grad_first = jnp.concatenate([results[stack_id][0][0][0] for stack_id in range(3)], axis=0)
    grad_hidden = jnp.stack(
        [
            jnp.stack([results[stack_id][0][layer_id][0] for layer_id in (1, 2, 3)])
            for stack_id in range(3)
        ]
    )
    grad_back = jnp.stack([results[stack_id][2][0] for stack_id in range(2)])
    grad_fore = jnp.concatenate([results[stack_id][1][0] for stack_id in range(3)], axis=1)
    bias_pieces = [results[stack_id][0][0][1] for stack_id in range(3)]
    bias_pieces += [
        results[stack_id][0][layer_id][1] for stack_id in range(3) for layer_id in (1, 2, 3)
    ]
    bias_pieces += [results[stack_id][2][1] for stack_id in range(2)]
    bias_pieces += [results[stack_id][1][1] for stack_id in range(3)]
    grad_bias = jnp.concatenate(bias_pieces)
    owned = (
        lax.psum_scatter(grad_first, "fsdp", scatter_dimension=1, tiled=True),
        lax.psum_scatter(grad_hidden, "fsdp", scatter_dimension=2, tiled=True),
        lax.psum_scatter(grad_back, "fsdp", scatter_dimension=1, tiled=True),
        lax.psum_scatter(grad_fore, "fsdp", scatter_dimension=0, tiled=True),
    )
    owned = lax.psum((owned[0], owned[1], owned[2], owned[3]), "dp")
    grad_bias, loss = lax.psum((grad_bias, loss_part), ("dp", "fsdp"))
    local_sq = sum((jnp.sum(grad * grad) for grad in owned))
    total_sq = lax.psum(local_sq, "fsdp") + jnp.sum(grad_bias * grad_bias)
    grad_norm = jnp.sqrt(total_sq)
    clip_factor = jnp.minimum(1.0, CLIP_MAX / grad_norm)
    step_float = step_count[0].astype(jnp.float32)
    states = (
        (first_w, first_w_avg, first_w_sq),
        (hidden_w, hidden_w_avg, hidden_w_sq),
        (back_w, back_w_avg, back_w_sq),
        (fore_w, fore_w_avg, fore_w_sq),
        (bias_vec, bias_avg, bias_sq),
    )
    grads_all = (owned[0], owned[1], owned[2], owned[3], grad_bias)
    updated = []
    for state, grad in zip(states, grads_all):
        updated.append(adamw(state[0], state[1], state[2], grad * clip_factor, step_float))
    return (
        loss,
        grad_norm,
        updated[0][0],
        updated[0][1],
        updated[0][2],
        updated[1][0],
        updated[1][1],
        updated[1][2],
        updated[2][0],
        updated[2][1],
        updated[2][2],
        updated[3][0],
        updated[3][1],
        updated[3][2],
        updated[4][0],
        updated[4][1],
        updated[4][2],
        updated[0][2].astype(jnp.bfloat16),
        updated[1][2].astype(jnp.bfloat16),
        updated[2][2].astype(jnp.bfloat16),
        updated[3][2].astype(jnp.bfloat16),
    )


def solution(mesh):
    placed = (
        P(("dp", "fsdp"), None),
        P(("dp", "fsdp"), None),
        P(("dp", "fsdp")),
        P(),
        P(None, "fsdp"),
        P(None, "fsdp"),
        P(None, "fsdp"),
        P(None, None, "fsdp", None),
        P(None, None, "fsdp", None),
        P(None, None, "fsdp", None),
        P(None, "fsdp", None),
        P(None, "fsdp", None),
        P(None, "fsdp", None),
        P("fsdp", None),
        P("fsdp", None),
        P("fsdp", None),
        P(),
        P(),
        P(),
    )
    return jax.shard_map(
        body,
        mesh=mesh,
        in_specs=placed,
        out_specs=(
            P(),
            P(),
            P(None, "fsdp"),
            P(None, "fsdp"),
            P(None, "fsdp"),
            P(None, None, "fsdp", None),
            P(None, None, "fsdp", None),
            P(None, None, "fsdp", None),
            P(None, "fsdp", None),
            P(None, "fsdp", None),
            P(None, "fsdp", None),
            P("fsdp", None),
            P("fsdp", None),
            P("fsdp", None),
            P(),
            P(),
            P(),
            P(None, "fsdp"),
            P(None, None, "fsdp", None),
            P(None, "fsdp", None),
            P("fsdp", None),
        ),
        check_vma=False,
    )
```

profile of v0, /device:TPU:0, one launch (start us, length us, event | category | flops | bytes accessed | tf_op | source)
XLA Modules:
  0.0 1032.2 jit_solution(3192349800689083075)
XLA Ops:
  13.0 42.4 %psum.56 = f32[]{:T(128)} all-reduce(f32[]{:T(128)} %convert_reduce_fusion.17), channel_id=1, replica_groups=mesh['dp'=4,'fsdp'=8] {'dp','fsdp'}, use_global_device_ids=true, to_apply=%region_6.7 | all-reduce | flops 1 | bytes 8 | tf_op jit(solution)/shard_map/psum | solution.py:165
  67.4 10.8 %subtract_divide_fusion = f32[864,3600]{1,0:T(8,128)} fusion(f32[864,3600]{1,0:T(8,128)} %param.25, f32[864]{0:T(1024)S(1)} %add_sqrt_fusion, f32[864]{0:T(1024)S(1)} %broadcast_multiply_fusion), kind=kLoop, calls=%fused_computation.9 | loop fusion | flops 6220800 | bytes 24890112 | tf_op jit(solution)/shard_map/div | solution.py:33
  78.2 14.2 %copy.126 = f32[864,3600]{0,1:T(8,128)} copy(f32[864,3600]{1,0:T(8,128)} %subtract_divide_fusion) | data formatting | bytes 24883200 | tf_op jit(solution)/shard_map/div | solution.py:33
  92.4 13.5 %all_gather.18 = bf16[512,810]{1,0:T(8,128)(2,1)} all-gather(bf16[64,810]{1,0:T(8,128)(2,1)S(1)} %convert_element_type.186), channel_id=1, replica_groups=mesh['dp'=4,'fsdp'=8] {'fsdp'}, dimensions={0}, use_global_device_ids=true | all-gather | bytes 933120 | tf_op jit(solution)/shard_map/all_gather | solution.py:176
  106.0 8.2 bitcast_reduce_fusion
  129.5 20.3 %all-gather.8.cloned.1.call-done = bf16[2,512,3600]{2,1,0:T(8,128)(2,1)} async-done(((bf16[2,64,3600]{2,1,0:T(8,128)(2,1)}), bf16[2,512,3600]{2,1,0:T(8,128)(2,1)}) %all-gather.8.cloned.1.call-update) | async-done | bytes 7372816 | tf_op jit(solution)/shard_map/all_gather | solution.py:175
  149.7 10.9 %add_subtract_fusion = f32[864,3600]{1,0:T(8,128)} fusion(f32[864,3600]{1,0:T(8,128)} %subtract_divide_fusion, bf16[864,512]{1,0:T(8,128)(2,1)S(1)} %get-tuple-element.126, f32[3600]{0:T(1024)S(1)} %get-tuple-element.125, bf16[2,512,3600]{2,1,0:T(8,128)(2,1)} %all-gather.8.cloned.1.call-done), kind=kOutput, calls=%fused_computation.7 | convolution fusion | flops 3191270400 | bytes 29970496 | tf_op jit(solution)/shard_map/dot_general | solution.py:97
  160.7 14.1 %copy.127 = f32[864,3600]{0,1:T(8,128)} copy(f32[864,3600]{1,0:T(8,128)} %add_subtract_fusion) | data formatting | bytes 24883200 | tf_op jit(solution)/shard_map/sub | solution.py:191
  174.8 15.1 %reshape.92 = f32[864,900,4]{0,2,1:T(4,128)} reshape(f32[864,3600]{0,1:T(8,128)} %copy.127) | data formatting | bytes 24883200 | tf_op jit(solution)/shard_map/reshape | solution.py:39
  189.9 10.3 %reduce_sum.255 = f32[864,900]{0,1:T(8,128)S(1)} reduce(f32[864,900,4]{0,2,1:T(4,128)} %reshape.92, f32[]{:T(128)} %constant.26.clone.1), dimensions={2}, to_apply=%region_3.0 | reduce | flops 2332800 | bytes 15552004 | tf_op jit(solution)/shard_map/reduce_sum | solution.py:39
  213.6 7.8 subtract_convert_fusion
  221.4 7.4 fusion.4
  237.3 7.7 fusion.7
  252.4 8.7 convert_reduce_fusion.2
  276.7 7.9 convolution_bitcast_fusion
  307.4 7.2 broadcast_in_dim.2
  314.6 15.4 %reshape.93 = f32[864,3600]{0,1:T(8,128)} reshape(f32[864,900,4]{0,2,1:T(4,128)} %broadcast_in_dim.2) | data formatting | bytes 24883200 | tf_op jit(solution)/shard_map/reshape | solution.py:46
  330.0 14.2 %copy.128 = f32[864,3600]{1,0:T(8,128)} copy(f32[864,3600]{0,1:T(8,128)} %reshape.93) | data formatting | bytes 24883200 | tf_op jit(solution)/shard_map/reshape | solution.py:46
  344.2 9.6 convert_reduce_fusion.1
  356.5 8.0 convolution_bitcast_fusion.1
  364.4 12.4 %pad_maximum_fusion = f32[2,512,3600]{1,2,0:T(8,128)} fusion(f32[1,512,3600]{1,2,0:T(8,128)} %convolution_bitcast_fusion, f32[1,512,3600]{1,2,0:T(8,128)} %convolution_bitcast_fusion.1), kind=kLoop, calls=%fused_computation | loop fusion | flops 3686400 | bytes 29491200 | tf_op jit(solution)/shard_map/stack | solution.py:232
  376.9 22.6 %copy.130 = f32[2,512,3600]{2,0,1:T(2,128)} copy(f32[2,512,3600]{1,2,0:T(8,128)} %pad_maximum_fusion) | data formatting | bytes 29491200 | tf_op jit(solution)/shard_map/stack | solution.py:232
  422.9 7.6 fusion
  461.6 25.2 %concatenate.9 = f32[4950,512]{1,0:T(8,128)} concatenate(f32[450,512]{1,0:T(8,128)S(1)} %copy-done.14, f32[900,512]{1,0:T(8,128)S(1)} %fusion.19, f32[3600,512]{1,0:T(8,128)} %fusion.55), dimensions={0} | concatenate | bytes 20275200 | tf_op jit(solution)/shard_map/concatenate | solution.py:225
  486.9 11.0 %copy.133 = f32[4950,512]{0,1:T(8,128)} copy(f32[4950,512]{1,0:T(8,128)} %concatenate.9) | data formatting | bytes 20275200
  499.8 100.8 %all-reduce.6.cloned.1.call-done = f32[2,512,3600]{2,0,1:T(2,128)} async-done(((f32[2,512,3600]{2,0,1:T(2,128)}), f32[2,512,3600]{2,0,1:T(2,128)}) %all-reduce.6.cloned.1.call-update) | async-done | bytes 14745616
  603.6 41.0 %reduce-scatter.12.cloned.1.call-done = f32[64,810]{1,0:T(8,128)} async-done(((f32[512,810]{1,0:T(8,128)}), f32[64,810]{1,0:T(8,128)}) %reduce-scatter.12.cloned.1.call-update) | async-done | bytes 207376 | tf_op jit(solution)/shard_map/reduce_scatter | solution.py:245
  644.6 80.3 %reduce-scatter.8.cloned.1.call-done = f32[3,3,64,512]{3,2,1,0:T(8,128)} async-done(((f32[3,3,512,512]{3,2,1,0:T(8,128)}), f32[3,3,64,512]{3,2,1,0:T(8,128)}) %reduce-scatter.8.cloned.1.call-update) | async-done | bytes 1179664 | tf_op jit(solution)/shard_map/reduce_scatter | solution.py:243
  724.9 84.2 %reduce-scatter.10.cloned.1.call-done = f32[64,4950]{1,0:T(8,128)} async-done(((f32[512,4950]{1,0:T(8,128)}), f32[64,4950]{1,0:T(8,128)}) %reduce-scatter.10.cloned.1.call-update) | async-done | bytes 1267216
  811.4 46.3 %all-reduce.1 = (f32[]{:T(128)}, f32[14154]{0:T(1024)S(1)}) all-reduce(f32[]{:T(128)S(6)} %div.181, f32[14154]{0:T(1024)S(1)} %concatenate.11), channel_id=1, replica_groups=mesh['dp'=4,'fsdp'=8] {'dp','fsdp'}, use_global_device_ids=true, to_apply=%region_7.8 | all-reduce | flops 14155 | bytes 113240 | tf_op jit(solution)/shard_map/psum | solution.py:248
  857.7 124.4 %all-reduce.8.cloned.1.call-done = (f32[4950,64]{0,1:T(8,128)}, f32[3,3,64,512]{3,2,1,0:T(8,128)}, f32[2,64,3600]{2,1,0:T(8,128)}, f32[64,810]{1,0:T(8,128)}) async-done(((f32[4950,64]{0,1:T(8,128)}, f32[3,3,64,512]{3,2,1,0:T(8,128)}, f32[2,64,3600]{2,1,0:T(8,128)}, f32[64,810]{1,0:T(8,128)}), (f32[4950,64]{0,1:T(8,128)}, f32[3,3,64,512]{3,2,1,0:T(8,128)}, f32[2,64,3600]{2,1,0:T(8,128)}, ...) | async-done | bytes 4497424 | tf_op jit(solution)/shard_map/psum | solution.py:247
  992.8 14.2 %psum.62 = f32[]{:T(128)} all-reduce(f32[]{:T(128)S(6)} %add.425), channel_id=1, replica_groups=mesh['dp'=4,'fsdp'=8] {'fsdp'}, use_global_device_ids=true, to_apply=%region_20.21 | all-reduce | flops 1 | bytes 8 | tf_op jit(solution)/shard_map/psum | solution.py:250
  (322 shorter events, 185.5 us)
Async XLA Ops:
  7.2 107.0 %all-gather.4.cloned.1.call-start = ((), (), s32[]{:S(2)}) async-start(), calls=%async_computation.3 | async-start | bytes 5750784 | tf_op jit(solution)/shard_map/all_gather | solution.py:173
  9.6 106.9 %all-gather.6.cloned.1.call-start = ((), (), s32[]{:S(2)}) async-start(), calls=%async_computation.4 | async-start | bytes 5308416 | tf_op jit(solution)/shard_map/all_gather | solution.py:174
  10.6 44.8 %copy-start.38 = (f32[14154]{0:T(1024)S(1)}, f32[14154]{0:T(1024)}, u32[]{:S(2)}) copy-start(f32[14154]{0:T(1024)} %param.41) | copy-start | bytes 169852
  10.6 45.0 %copy-start.36 = (f32[64,810]{1,0:T(8,128)S(1)}, f32[64,810]{1,0:T(8,128)}, u32[]{:S(2)}) copy-start(f32[64,810]{1,0:T(8,128)} %param.38) | copy-start | bytes 622084
  10.6 139.1 %all-gather.8.cloned.1.call-start = ((), (), s32[]{:S(2)}) async-start(), calls=%async_computation.5 | async-start | bytes 8552448 | tf_op jit(solution)/shard_map/all_gather | solution.py:175
  12.3 588.3 %all-reduce.6.cloned.1.call-start = ((), (), s32[]{:S(2)}) async-start(), calls=%async_computation.9 | async-start | bytes 30408704
  105.9 10.6 %copy-start.47 = (f32[512]{0:T(512)}, f32[512]{0:T(512)S(1)}, u32[]{:S(2)}) copy-start(f32[512]{0:T(512)S(1)} %get-tuple-element.123) | copy-start | bytes 6148
  105.9 12.7 %copy-start.49 = (f32[512]{0:T(512)}, f32[512]{0:T(512)S(1)}, u32[]{:S(2)}) copy-start(f32[512]{0:T(512)S(1)} %get-tuple-element.122) | copy-start | bytes 6148
  105.9 14.7 %copy-start.51 = (f32[512]{0:T(512)}, f32[512]{0:T(512)S(1)}, u32[]{:S(2)}) copy-start(f32[512]{0:T(512)S(1)} %get-tuple-element.121) | copy-start | bytes 6148
  105.9 14.7 %copy-start.53 = (f32[512]{0:T(512)}, f32[512]{0:T(512)S(1)}, u32[]{:S(2)}) copy-start(f32[512]{0:T(512)S(1)} %get-tuple-element.120) | copy-start | bytes 6148
  124.4 25.4 %copy-start.15 = (bf16[864,512]{1,0:T(8,128)(2,1)}, bf16[864,512]{1,0:T(8,128)(2,1)S(1)}, u32[]{:S(2)}) copy-start(bf16[864,512]{1,0:T(8,128)(2,1)S(1)} %get-tuple-element.126) | copy-start | bytes 2654212
  228.8 41.1 %copy-start.82 = (f32[864,512]{1,0:T(8,128)}, f32[864,512]{1,0:T(8,128)S(1)}, u32[]{:S(2)}) copy-start(f32[864,512]{1,0:T(8,128)S(1)} %fusion.4) | copy-start | bytes 5308420
  230.9 35.9 %copy-start.84 = (f32[864,512]{1,0:T(8,128)}, f32[864,512]{1,0:T(8,128)S(1)}, u32[]{:S(2)}) copy-start(f32[864,512]{1,0:T(8,128)S(1)} %fusion.28) | copy-start | bytes 5308420
  232.9 30.8 %copy-start.86 = (f32[864,512]{1,0:T(8,128)}, f32[864,512]{1,0:T(8,128)S(1)}, u32[]{:S(2)}) copy-start(f32[864,512]{1,0:T(8,128)S(1)} %fusion.29) | copy-start | bytes 5308420
  235.0 26.0 %copy-start.70 = (f32[864,512]{1,0:T(8,128)}, f32[864,512]{1,0:T(8,128)S(1)}, u32[]{:S(2)}) copy-start(f32[864,512]{1,0:T(8,128)S(1)} %fusion.30) | copy-start | bytes 5308420
  237.3 7.7 copy-start.18
  237.3 7.7 copy-start.64
  237.3 7.7 copy-start.65
  276.7 7.9 copy-start.2
  344.2 12.3 %copy-start.16 = (bf16[864,512]{1,0:T(8,128)(2,1)S(1)}, bf16[864,512]{1,0:T(8,128)(2,1)}, u32[]{:S(2)}) copy-start(bf16[864,512]{1,0:T(8,128)(2,1)} %copy-done.15) | copy-start | bytes 2654212
  399.5 245.1 %reduce-scatter.12.cloned.1.call-start = ((), (), s32[]{:S(2)}) async-start(), calls=%async_computation.8 | async-start | bytes 2064384 | tf_op jit(solution)/shard_map/reduce_scatter | solution.py:245
  422.8 7.7 copy-start.54
  422.8 302.1 %reduce-scatter.8.cloned.1.call-start = ((), (), s32[]{:S(2)}) async-start(), calls=%async_computation.6 | async-start | bytes 10616832 | tf_op jit(solution)/shard_map/reduce_scatter | solution.py:243
  448.2 360.9 %reduce-scatter.10.cloned.1.call-start = ((), (), s32[]{:S(2)}) async-start(), calls=%async_computation.7 | async-start | bytes 11501568
  497.9 484.1 %all-reduce.8.cloned.1.call-start = ((), (), s32[]{:S(2)}) async-start(), calls=%async_computation.10 | async-start | bytes 9175040 | tf_op jit(solution)/shard_map/psum | solution.py:247
  983.7 24.6 %copy-start.39 = (f32[14154]{0:T(1024)S(1)}, f32[14154]{0:T(1024)}, u32[]{:S(2)}) copy-start(f32[14154]{0:T(1024)} %param.41) | copy-start | bytes 169852
  983.8 24.6 %copy-start.44 = (f32[14154]{0:T(1024)S(1)}, f32[14154]{0:T(1024)}, u32[]{:S(2)}) copy-start(f32[14154]{0:T(1024)} %param.43) | copy-start | bytes 169852
  986.4 23.6 %copy-start.35 = (f32[64,810]{1,0:T(8,128)S(1)}, f32[64,810]{1,0:T(8,128)}, u32[]{:S(2)}) copy-start(f32[64,810]{1,0:T(8,128)} %get-tuple-element.89) | copy-start | bytes 622084
  986.4 23.6 %copy-start.37 = (f32[64,810]{1,0:T(8,128)S(1)}, f32[64,810]{1,0:T(8,128)}, u32[]{:S(2)}) copy-start(f32[64,810]{1,0:T(8,128)} %param.38) | copy-start | bytes 622084
  986.4 23.6 %copy-start.40 = (f32[64,810]{1,0:T(8,128)S(1)}, f32[64,810]{1,0:T(8,128)}, u32[]{:S(2)}) copy-start(f32[64,810]{1,0:T(8,128)} %param.40) | copy-start | bytes 622084
  986.4 23.6 %copy-start.41 = (f32[64,810]{1,0:T(8,128)S(1)}, f32[64,810]{1,0:T(8,128)}, u32[]{:S(2)}) copy-start(f32[64,810]{1,0:T(8,128)} %param.39) | copy-start | bytes 622084
  988.6 22.3 %copy-start.12 = (f32[3,3,64,512]{3,2,1,0:T(8,128)S(1)}, f32[3,3,64,512]{3,2,1,0:T(8,128)}, u32[]{:S(2)}) copy-start(f32[3,3,64,512]{3,2,1,0:T(8,128)} %param.32) | copy-start | bytes 3538948
  (86 other events, 266.5 us)
Sparse Core Ops, SparseCore 0:
  10.5 43.9 all-gather.3
  57.0 39.1 all-gather.5
  98.6 51.0 all-gather.7
  399.6 200.9 all-reduce.5
  604.8 39.7 reduce-scatter.11
  648.4 76.4 reduce-scatter.7
  728.9 80.0 reduce-scatter.9
  812.3 169.7 all-reduce.7
where the time goes:
time: 1040 us; the launch traced here: 1030 us
  waiting for transfers between devices  451 us (43%)
  matrix products  186 us (18%)
  local copies, waits for them, and re-layouts  159 us (15%)
  blocking collectives  116 us (11%)
  other arithmetic  96.2 us (9%)
  between operations  23.4 us (2%)
    unnamed x10, waiting for transfers between devices  185 us
    psum x1, waiting for transfers between devices, body(): owned = lax.psum((owned[0], owned[1], owned[2], owned[3]), 'dp')  124 us
    reduce_scatter x1, waiting for transfers between devices, body(): lax.psum_scatter(grad_hidden, 'fsdp', scatter_dimension=2, tiled=True)  80.3 us
    psum x1, blocking collectives, body(): grad_bias, loss = lax.psum((grad_bias, loss_part), ('dp', 'fsdp'))  46.3 us
    psum x1, blocking collectives, body(): lax.psum(jnp.sum(horizon.astype(jnp.float32)), ('dp', 'fsdp'))  42.4 us
    reduce_scatter x1, waiting for transfers between devices, body(): lax.psum_scatter(grad_fore, 'fsdp', scatter_dimension=0, tiled=True)  41 us
    dot_general x12, matrix products, stack_forward(): jnp.dot(inputs_kept[-1], weight, preferred_element_type=jnp.float32) + bias  36.3 us
    dot_general x11, matrix products, stack_backward(): jnp.dot(d_pre, layers[layer_id][0].T, preferred_element_type=jnp.float32)  32.7 us
  transfers between devices with their start and end apart: 8, of which 6 were waited for; matrix products, arithmetic and copies ran while one was open for 15% of the time, Pallas kernels for 0%

commit v1 on v0

--- a/solution.py
+++ b/solution.py
@@ -1,7 +1,10 @@
+import functools
 import jax
 import jax.numpy as jnp
 import numpy as np
 from jax import lax
+from jax.experimental import pallas as pl
+from jax.experimental.pallas import tpu as pltpu
 from jax.sharding import PartitionSpec as P
 
 KERNELS = (8, 4, 1)
@@ -287,7 +290,578 @@
     )
 
 
+MESH = pl.DeviceIdType.MESH
+CHUNK = 1024
+
+
+def tiled(width):
+    return -(-width // 128) * 128
+
+
+def packing(length, steps_ahead_total, hidden_size):
+    pieces = {}
+    cursor = 0
+    for stack_id in range(3):
+        widths = [("first", length // KERNELS[stack_id])]
+        widths += [(layer_id, hidden_size) for layer_id in range(3)]
+        if stack_id < 2:
+            widths.append(("back", length))
+        widths.append(("fore", steps_ahead_total // RATIOS[stack_id]))
+        for name, width in widths:
+            pieces[stack_id, name] = (cursor, width)
+            cursor += tiled(width)
+    total = -(-cursor // CHUNK) * CHUNK
+    return pieces, total
+
+
+def pack(parts, pieces, total):
+    out = []
+    cursor = 0
+    for key, (start, width) in pieces.items():
+        part = parts[key]
+        out.append(jnp.pad(part, ((0, 0), (0, tiled(width) - width))))
+        cursor = start + tiled(width)
+    rows, dtype = out[0].shape[0], out[0].dtype
+    if total > cursor:
+        out.append(jnp.zeros((rows, total - cursor), dtype))
+    return jnp.concatenate(out, axis=1)
+
+
+def places():
+    row = lax.axis_index("dp")
+    me = lax.axis_index("fsdp")
+    core = me % 2
+    across_x = (me // 2) % 2
+    across_y = me // 4
+    other = me + 1 - 2 * core
+    over_x = me + 2 - 4 * across_x
+    over_y = me + 4 - 8 * across_y
+    return row, me, core, other, over_x, over_y
+
+
+def remote(src, dst, send_sem, recv_sem, device):
+    return pltpu.make_async_remote_copy(
+        src_ref=src, dst_ref=dst, send_sem=send_sem, recv_sem=recv_sem, device_id=device, device_id_type=MESH
+    )
+
+
+def gather_kernel(cuts, shard_ref, full_ref, own_sem, send_sem, recv_sem):
+    row, me, core, other, over_x, over_y = places()
+    diag = over_x + over_y - me
+    barrier = pltpu.get_barrier_semaphore()
+    for peer in (other, over_x, over_y):
+        pl.semaphore_signal(barrier, inc=1, device_id=(row, peer), device_id_type=MESH)
+    pl.semaphore_wait(barrier, 3)
+    own = pltpu.make_async_copy(shard_ref, full_ref.at[me], own_sem)
+    own.start()
+    sends = []
+
+    def send(kind, part, src, block, device):
+        start, width = cuts[part]
+        copy = remote(
+            src.at[:, start : start + width],
+            full_ref.at[block, :, start : start + width],
+            send_sem.at[kind, part],
+            recv_sem.at[kind, part],
+            (row, device),
+        )
+        copy.start()
+        sends.append(copy)
+        return copy
+
+    count = len(cuts)
+    via_x = [None] * count
+    via_y = [None] * count
+    local = []
+    for part in range(count):
+        via_x[part] = send(0, part, shard_ref, me, over_x)
+        via_y[part] = send(1, part, shard_ref, me, over_y)
+        local.append(send(2, part, shard_ref, me, other))
+    for part in range(count):
+        via_x[part].wait_recv()
+        local.append(send(3, part, full_ref.at[over_x], over_x, other))
+        if part % 2 == 0:
+            onward = send(6, part, full_ref.at[over_x], over_x, over_y)
+        via_y[part].wait_recv()
+        local.append(send(4, part, full_ref.at[over_y], over_y, other))
+        if part % 2 == 1:
+            onward = send(6, part, full_ref.at[over_y], over_y, over_x)
+        onward.wait_recv()
+        local.append(send(5, part, full_ref.at[diag], diag, other))
+    for copy in local:
+        copy.wait_recv()
+    for copy in sends:
+        copy.wait_send()
+    own.wait()
+
+
+def gather(shard, cuts):
+    rows, total = shard.shape
+    count = len(cuts)
+    return pl.pallas_call(
+        functools.partial(gather_kernel, cuts),
+        out_shape=jax.ShapeDtypeStruct((8, rows, total), shard.dtype),
+        in_specs=[pl.BlockSpec(memory_space=pltpu.HBM)],
+        out_specs=pl.BlockSpec(memory_space=pltpu.HBM),
+        scratch_shapes=[
+            pltpu.SemaphoreType.DMA,
+            pltpu.SemaphoreType.DMA((7, count)),
+            pltpu.SemaphoreType.DMA((7, count)),
+        ],
+        compiler_params=pltpu.CompilerParams(collective_id=0, has_side_effects=True),
+        name="gather_weights",
+    )(shard)
+
+
+def reduce_kernel(
+    count, grad_ref, small_ref, out_ref, small_out_ref, square_ref,
+    mine, from_core, s1, r1, keep, s2, r2, plane, zs, zr, zp_s, zp_r, final,
+    small_s, small_r, square_s, square_r,
+    load_sem, core_ss, core_rs, ss1, rs1, ss2, rs2, zss, zrs, pss, prs, fss, frs, small_ss, small_rs, sq_ss, sq_rs, out_sem,
+):
+    row, me, core, other, over_x, over_y = places()
+    lane = core
+    chip = me // 2
+    chip_x = over_x // 2
+    chip_y = over_y // 2
+    chip_d = chip_x + chip_y - chip
+    half = CHUNK // 2
+    rows = grad_ref.shape[2]
+    z_out = jnp.where(row < 2, row - 1, row + 1)
+    z_out = jnp.clip(z_out, 0, 3)
+    z_in = jnp.where(row < 2, row + 1, row - 1)
+    middle = (row == 1) | (row == 2)
+
+    barrier = pltpu.get_barrier_semaphore()
+    for peer in range(1, 8):
+        pl.semaphore_signal(barrier, inc=1, device_id=(row, (me + peer) % 8), device_id_type=MESH)
+    for peer in range(1, 4):
+        pl.semaphore_signal(barrier, inc=1, device_id=((row + peer) % 4, me), device_id_type=MESH)
+    pl.semaphore_wait(barrier, 10)
+
+    def columns(t):
+        return pl.ds(pl.multiple_of(t * CHUNK, CHUNK), CHUNK)
+
+    def load(t):
+        return pltpu.make_async_copy(grad_ref.at[:, lane, :, columns(t)], mine.at[t % 2], load_sem.at[t % 2])
+
+    def core_copy(t):
+        return remote(
+            grad_ref.at[:, 1 - lane, :, columns(t)], from_core.at[t], core_ss.at[t], core_rs.at[t], (row, other)
+        )
+
+    def first_x(t):
+        return remote(s1.at[t, 0], r1.at[t, 0], ss1.at[t, 0], rs1.at[t, 0], (row, over_x))
+
+    def first_y(t):
+        return remote(s1.at[t, 1], r1.at[t, 1], ss1.at[t, 1], rs1.at[t, 1], (row, over_y))
+
+    def second_y(t):
+        return remote(s2.at[t, 0], r2.at[t, 0], ss2.at[t, 0], rs2.at[t, 0], (row, over_y))
+
+    def second_x(t):
+        return remote(s2.at[t, 1], r2.at[t, 1], ss2.at[t, 1], rs2.at[t, 1], (row, over_x))
+
+    def z_all(t):
+        return remote(zs.at[t], zr.at[t], zss.at[t], zrs.at[t], (z_in, me))
+
+    def z_part(t):
+        return remote(zp_s.at[t], zp_r.at[t], pss.at[t], prs.at[t], (z_in, me))
+
+    def z_final(t, piece, way, device):
+        return remote(final.at[t, piece], final.at[t, piece], fss.at[t, way], frs.at[t, piece], (device, me))
+
+    near = jnp.where(row < 2, 0, 1)
+
+    def stage_one(t):
+        load(t).wait()
+
+        @pl.when(t + 1 < count)
+        def _():
+            load(t + 1).start()
+
+        core_copy(t).wait_recv()
+        slot = t % 4
+        for way, chips in ((0, (chip_x, chip_d)), (1, (chip_y, chip_d))):
+            cols = slice(way * half, way * half + half)
+            for k, c in enumerate(chips):
+                s1[t, way, k] = (mine[t % 2, c, :, cols] + from_core[t, c, :, cols]).astype(jnp.bfloat16)
+            (first_x, first_y)[way](t).start()
+        for way, chips in ((0, (chip, chip_y)), (1, (chip, chip_x))):
+            cols = slice(way * half, way * half + half)
+            for k, c in enumerate(chips):
+                keep[slot, way, k] = mine[t % 2, c, :, cols] + from_core[t, c, :, cols]
+
+    def stage_two(t):
+        slot = t % 4
+        for way, copy, onward in ((0, first_x, second_y), (1, first_y, second_x)):
+            copy(t).wait_recv()
+            s2[t, way] = (keep[slot, way, 1] + r1[t, way, 1].astype(jnp.float32)).astype(jnp.bfloat16)
+            onward(t).start()
+            keep[slot, way, 0] = keep[slot, way, 0] + r1[t, way, 0].astype(jnp.float32)
+
+    def stage_three(t):
+        slot = t % 4
+        for way, copy in ((0, second_y), (1, second_x)):
+            copy(t).wait_recv()
+            total = keep[slot, way, 0] + r2[t, way].astype(jnp.float32)
+            plane[slot, way] = total
+            zs[t, way] = total.astype(jnp.bfloat16)
+
+        @pl.when(jnp.logical_not(middle))
+        def _():
+            z_all(t).start()
+
+    def stage_four(t):
+        @pl.when(middle)
+        def _():
+            slot = t % 4
+            z_all(t).wait_recv()
+            plane[slot, 0] = plane[slot, 0] + zr[t, 0].astype(jnp.float32)
+            plane[slot, 1] = plane[slot, 1] + zr[t, 1].astype(jnp.float32)
+            zp_s[t] = plane[slot, 1 - near].astype(jnp.bfloat16)
+            z_part(t).start()
+
+    def stage_five(t):
+        @pl.when(middle)
+        def _():
+            slot = t % 4
+            z_part(t).wait_recv()
+            final[t, near] = (plane[slot, near] + zp_r[t].astype(jnp.float32)).astype(jnp.bfloat16)
+            z_final(t, near, 0, z_in).start()
+            z_final(t, near, 1, z_out).start()
+
+    def stage_six(t):
+        @pl.when(middle)
+        def _():
+            z_final(t, 1 - near, 2, z_out).wait_recv()
+            z_final(t, 1 - near, 2, z_out).start()
+
+        @pl.when(jnp.logical_not(middle))
+        def _():
+            z_final(t, 0, 0, z_in).wait_recv()
+            z_final(t, 1, 1, z_in).wait_recv()
+
+        pltpu.make_async_copy(final.at[t], out_ref.at[t], out_sem).start()
+        got = final[t].astype(jnp.float32)
+        got = got * got
+        got = got[0] + got[1]
+        acc = square_s[...]
+        for k in range(0, rows, 8):
+            for j in range(0, half, 128):
+                acc = acc + got[k : k + 8, j : j + 128]
+        square_s[...] = acc
+
+    row_pair = row + 1 - 2 * (row % 2)
+    row_far = row + 2 - 4 * (row // 2)
+    hops = ((row, other), (row, over_x), (row, over_y), (row_pair, me), (row_far, me))
+
+    def small_step(k):
+        return remote(small_s.at[k], small_r.at[k], small_ss.at[k], small_rs.at[k], hops[k])
+
+    def small_stage(k):
+        if k == 0:
+            small_s[0] = small_ref[...]
+        else:
+            small_step(k - 1).wait_recv()
+            total = small_s[k - 1] + small_r[k - 1]
+            if k < len(hops):
+                small_s[k] = total
+            else:
+                small_out_ref[...] = total
+        if k < len(hops):
+            small_step(k).start()
+
+    square_s[...] = jnp.zeros_like(square_s)
+    load(0).start()
+
+    def start_core(t, carry):
+        core_copy(t).start()
+        return carry
+
+    lax.fori_loop(0, count, start_core, 0)
+
+    def turn(t, carry):
+        for lag, stage in ((0, stage_one), (1, stage_two), (2, stage_three), (3, stage_four), (4, stage_five), (5, stage_six)):
+            @pl.when((t >= lag) & (t < count + lag))
+            def _():
+                stage(t - lag)
+
+        for k in range(len(hops) + 1):
+            @pl.when(t == 2 + 2 * k)
+            def _():
+                small_stage(k)
+        return carry
+
+    lax.fori_loop(0, count + 5, turn, 0)
+
+    def square_copy(peer):
+        device = (me + peer) % 8
+        return remote(square_s, square_r.at[me], sq_ss.at[peer], sq_rs.at[peer], (row, device))
+
+    def square_wait(peer):
+        device = (me - peer + 8) % 8
+        return remote(square_s, square_r.at[device], sq_ss.at[peer], sq_rs.at[peer], (row, device))
+
+    for peer in range(1, 8):
+        square_copy(peer).start()
+    square_r[me] = square_s[...]
+    for peer in range(1, 8):
+        square_wait(peer).wait_recv()
+    acc = square_r[0]
+    for block in range(1, 8):
+        acc = acc + square_r[block]
+    square_ref[...] = acc
+
+    def finish(t, carry):
+        core_copy(t).wait_send()
+        first_x(t).wait_send()
+        first_y(t).wait_send()
+        second_x(t).wait_send()
+        second_y(t).wait_send()
+
+        @pl.when(middle)
+        def _():
+            z_part(t).wait_send()
+            z_final(t, near, 0, z_in).wait_send()
+            z_final(t, near, 1, z_out).wait_send()
+            z_final(t, 1 - near, 2, z_out).wait_send()
+
+        @pl.when(jnp.logical_not(middle))
+        def _():
+            z_all(t).wait_send()
+
+        pltpu.make_async_copy(final.at[t], out_ref.at[t], out_sem).wait()
+        return carry
+
+    lax.fori_loop(0, count, finish, 0)
+    for k in range(len(hops)):
+        small_step(k).wait_send()
+    for peer in range(1, 8):
+        square_copy(peer).wait_send()
+
+
+def reduce_grads(grads, small):
+    _, _, rows, total = grads.shape
+    count = total // CHUNK
+    half = CHUNK // 2
+    low, wide = jnp.bfloat16, jnp.float32
+    dma = pltpu.SemaphoreType.DMA
+    return pl.pallas_call(
+        functools.partial(reduce_kernel, count),
+        out_shape=(
+            jax.ShapeDtypeStruct((count, 2, rows, half), low),
+            jax.ShapeDtypeStruct(small.shape, wide),
+            jax.ShapeDtypeStruct((8, 128), wide),
+        ),
+        in_specs=[pl.BlockSpec(memory_space=pltpu.HBM), pl.BlockSpec(memory_space=pltpu.VMEM)],
+        out_specs=(
+            pl.BlockSpec(memory_space=pltpu.HBM),
+            pl.BlockSpec(memory_space=pltpu.VMEM),
+            pl.BlockSpec(memory_space=pltpu.VMEM),
+        ),
+        scratch_shapes=[
+            pltpu.VMEM((2, 4, rows, CHUNK), wide),
+            pltpu.VMEM((count, 4, rows, CHUNK), wide),
+            pltpu.VMEM((count, 2, 2, rows, half), low),
+            pltpu.VMEM((count, 2, 2, rows, half), low),
+            pltpu.VMEM((4, 2, 2, rows, half), wide),
+            pltpu.VMEM((count, 2, rows, half), low),
+            pltpu.VMEM((count, 2, rows, half), low),
+            pltpu.VMEM((4, 2, rows, half), wide),
+            pltpu.VMEM((count, 2, rows, half), low),
+            pltpu.VMEM((count, 2, rows, half), low),
+            pltpu.VMEM((count, rows, half), low),
+            pltpu.VMEM((count, rows, half), low),
+            pltpu.VMEM((count, 2, rows, half), low),
+            pltpu.VMEM((5,) + small.shape, wide),
+            pltpu.VMEM((5,) + small.shape, wide),
+            pltpu.VMEM((8, 128), wide),
+            pltpu.VMEM((8, 8, 128), wide),
+            dma((2,)),
+            dma((count,)),
+            dma((count,)),
+            dma((count, 2)),
+            dma((count, 2)),
+            dma((count, 2)),
+            dma((count, 2)),
+            dma((count,)),
+            dma((count,)),
+            dma((count,)),
+            dma((count,)),
+            dma((count, 3)),
+            dma((count, 2)),
+            dma((5,)),
+            dma((5,)),
+            dma((8,)),
+            dma((8,)),
+            dma,
+        ],
+        compiler_params=pltpu.CompilerParams(
+            collective_id=1, has_side_effects=True, vmem_limit_bytes=60 * 1024 * 1024
+        ),
+        name="reduce_grads",
+    )(grads, small)
+
+
+def fast_body(
+    devices,
+    windows,
+    targets,
+    horizon,
+    step_count,
+    first_w,
+    first_w_avg,
+    first_w_sq,
+    hidden_w,
+    hidden_w_avg,
+    hidden_w_sq,
+    back_w,
+    back_w_avg,
+    back_w_sq,
+    fore_w,
+    fore_w_avg,
+    fore_w_sq,
+    bias_vec,
+    bias_avg,
+    bias_sq,
+):
+    length = windows.shape[1]
+    steps_ahead_total = targets.shape[1]
+    hidden_size = hidden_w.shape[-1]
+    pieces, total = packing(length, steps_ahead_total, hidden_size)
+
+    def split(first, hidden, back, fore, stack_id):
+        row_start = sum(length // KERNELS[earlier] for earlier in range(stack_id))
+        col_start = sum(steps_ahead_total // RATIOS[earlier] for earlier in range(stack_id))
+        parts = {(stack_id, "first"): first[row_start : row_start + length // KERNELS[stack_id]].T}
+        for layer_id in range(3):
+            parts[stack_id, layer_id] = hidden[stack_id, layer_id]
+        if stack_id < 2:
+            parts[stack_id, "back"] = back[stack_id]
+        parts[stack_id, "fore"] = fore[:, col_start : col_start + steps_ahead_total // RATIOS[stack_id]]
+        return parts
+
+    low = jnp.bfloat16
+    parts = {}
+    for stack_id in range(3):
+        parts.update(split(first_w.astype(low), hidden_w.astype(low), back_w.astype(low), fore_w.astype(low), stack_id))
+    shard = pack(parts, pieces, total)
+    cuts = []
+    for stack_id in range(3):
+        for names in (("first", 0, 1, 2), ("back", "fore")):
+            names = [name for name in names if (stack_id, name) in pieces]
+            start = pieces[stack_id, names[0]][0]
+            stop = pieces[stack_id, names[-1]][0] + tiled(pieces[stack_id, names[-1]][1])
+            cuts.append((start, stop - start))
+    full = gather(shard, tuple(cuts)).reshape(hidden_size, total)
+
+    def piece(key):
+        start, width = pieces[key]
+        return full[:, start : start + width]
+
+    normed, observed_future = normalize(windows, targets)
+    flags = (jnp.arange(steps_ahead_total, dtype=jnp.int32)[None, :] < horizon[:, None]).astype(jnp.float32)
+    tally = jnp.sum(horizon.astype(jnp.float32))
+    residual = normed
+    kept_stacks = []
+    stack_args = []
+    predicted_future = jnp.zeros(observed_future.shape, jnp.float32)
+    for stack_id in range(3):
+        layers = [(piece((stack_id, "first")).T, bias_vec[stack_id * hidden_size : (stack_id + 1) * hidden_size])]
+        for layer_id in range(3):
+            offset = (3 + 3 * stack_id + layer_id) * hidden_size
+            layers.append((piece((stack_id, layer_id)), bias_vec[offset : offset + hidden_size]))
+        col_start = sum(steps_ahead_total // RATIOS[earlier] for earlier in range(stack_id))
+        fore_start = 12 * hidden_size + 2 * length + col_start
+        anchor_entries = steps_ahead_total // RATIOS[stack_id]
+        fore_pair = (piece((stack_id, "fore")), bias_vec[fore_start : fore_start + anchor_entries])
+        back_pair = None
+        if stack_id < 2:
+            back_start = 12 * hidden_size + stack_id * length
+            back_pair = (piece((stack_id, "back")), bias_vec[back_start : back_start + length])
+        upsample = jnp.asarray(blend_coefficients(steps_ahead_total, anchor_entries))
+        stack_args.append((layers, fore_pair, back_pair, upsample))
+        kept, running_subtotal, backcast = stack_forward(residual, stack_id, *stack_args[-1])
+        kept_stacks.append(kept)
+        predicted_future = predicted_future + running_subtotal
+        if backcast is not None:
+            residual = residual - backcast
+    difference = predicted_future - observed_future
+    loss_part = jnp.sum(flags * difference * difference)
+    scale = 2.0 ** -int(np.ceil(np.log2(devices * windows.shape[0] * steps_ahead_total)))
+    cotangent = (2.0 * scale) * flags * difference
+    results = [None, None, None]
+    d_residual = None
+    for stack_id in (2, 1, 0):
+        layers, fore_pair, back_pair, upsample = stack_args[stack_id]
+        anchor_cotangent = jnp.dot(cotangent, upsample.T, precision=DOT_EXACTNESS)
+        d_backcast = None if d_residual is None else -d_residual
+        results[stack_id] = stack_backward(
+            kept_stacks[stack_id], anchor_cotangent, d_backcast, layers, fore_pair, back_pair, stack_id > 0
+        )
+        if stack_id > 0:
+            spread_back = pool_back(results[stack_id][3], KERNELS[stack_id])
+            d_residual = spread_back if d_residual is None else d_residual + spread_back
+    parts = {}
+    for stack_id in range(3):
+        parts[stack_id, "first"] = results[stack_id][0][0][0].T
+        for layer_id in range(3):
+            parts[stack_id, layer_id] = results[stack_id][0][layer_id + 1][0]
+        if stack_id < 2:
+            parts[stack_id, "back"] = results[stack_id][2][0]
+        parts[stack_id, "fore"] = results[stack_id][1][0]
+    grads = pack(parts, pieces, total)
+    bias_pieces = [results[stack_id][0][0][1] for stack_id in range(3)]
+    bias_pieces += [results[stack_id][0][layer_id][1] for stack_id in range(3) for layer_id in (1, 2, 3)]
+    bias_pieces += [results[stack_id][2][1] for stack_id in range(2)]
+    bias_pieces += [results[stack_id][1][1] for stack_id in range(3)]
+    bias_count = bias_vec.shape[0]
+    small_rows = -(-(bias_count + 2) // 1024) * 8
+    small = jnp.concatenate(bias_pieces + [jnp.stack([loss_part, tally])])
+    small = jnp.pad(small, (0, small_rows * 128 - small.shape[0])).reshape(small_rows, 128)
+    grads = grads.reshape(4, 2, hidden_size // 8, total)
+    owned, small, square = reduce_grads(grads, small)
+    owned = owned.transpose(2, 0, 1, 3).reshape(hidden_size // 8, total)
+    small = small.reshape(-1)
+    grad_bias, loss_sum, tally = small[:bias_count], small[bias_count], small[bias_count + 1]
+    factor = 1.0 / (scale * tally)
+    loss = loss_sum / tally
+    grad_norm = jnp.sqrt(jnp.sum(square) + jnp.sum(grad_bias * grad_bias)) * factor
+    clip_factor = jnp.minimum(1.0, CLIP_MAX / grad_norm) * factor
+    step_float = step_count[0].astype(jnp.float32)
+
+    def grad_piece(key):
+        start, width = pieces[key]
+        return owned[:, start : start + width].astype(jnp.float32)
+
+    grads_all = (
+        jnp.concatenate([grad_piece((stack_id, "first")) for stack_id in range(3)], axis=1).T,
+        jnp.stack([jnp.stack([grad_piece((stack_id, layer_id)) for layer_id in range(3)]) for stack_id in range(3)]),
+        jnp.stack([grad_piece((stack_id, "back")) for stack_id in range(2)]),
+        jnp.concatenate([grad_piece((stack_id, "fore")) for stack_id in range(3)], axis=1),
+        grad_bias,
+    )
+    states = (
+        (first_w, first_w_avg, first_w_sq),
+        (hidden_w, hidden_w_avg, hidden_w_sq),
+        (back_w, back_w_avg, back_w_sq),
+        (fore_w, fore_w_avg, fore_w_sq),
+        (bias_vec, bias_avg, bias_sq),
+    )
+    updated = []
+    for state, grad in zip(states, grads_all):
+        updated.append(adamw(state[0], state[1], state[2], grad * clip_factor, step_float))
+    flat = [loss, grad_norm]
+    for triple in updated:
+        flat.extend(triple)
+    flat += [triple[2].astype(low) for triple in updated[:4]]
+    return tuple(flat)
+
+
 def solution(mesh):
+    fast = mesh.shape["fsdp"] == 8 and mesh.shape["dp"] == 4
+    step = functools.partial(fast_body, mesh.shape["dp"] * mesh.shape["fsdp"]) if fast else body
     placed = (
         P(("dp", "fsdp"), None),
         P(("dp", "fsdp"), None),
@@ -310,7 +884,7 @@
         P(),
     )
     return jax.shard_map(
-        body,
+        step,
         mesh=mesh,
         in_specs=placed,
         out_specs=(

time: 1040 us -> 686 us (0.66)
  waiting for transfers between devices: 451 us -> 0 us
  Pallas kernels: 0 us -> 235 us
  blocking collectives: 116 us -> 0 us
  between operations: 23.4 us -> 8.63 us
  other arithmetic: 96.2 us -> 83 us
  local copies, waits for them, and re-layouts: 159 us -> 170 us
    pallas_call x0 -> x2, Pallas kernels: none -> 235 us  [the longest x1 123 us: reduce_grads(): pl.pallas_call(functools.partial(reduce_kernel, count), out_shape=(jax.Sh...]
    unnamed x10 -> x0, waiting for transfers between devices: 185 us -> none
    psum x1 -> x0, waiting for transfers between devices: 124 us -> none  [body(): owned = lax.psum((owned[0], owned[1], owned[2], owned[3]), 'dp')]
    reduce_scatter x2 -> x0, waiting for transfers between devices: 121 us -> none  [the longest x1 80.3 us: body(): lax.psum_scatter(grad_hidden, 'fsdp', scatter_dimension=2, tiled=True)]
    psum x3 -> x0, blocking collectives: 103 us -> none  [the longest x1 46.3 us: body(): grad_bias, loss = lax.psum((grad_bias, loss_part), ('dp', 'fsdp'))]
    all_gather x3 -> x0, waiting for transfers between devices: 20.3 us -> none  [the longest x1 20.3 us: body(): lax.all_gather(shards[2], 'fsdp', axis=1, tiled=True)]
    another operation x1 -> x2, local copies, waits for them, and re-layouts: 22.6 us -> 3.37 us  [the longest x1 2.22 us: fast_body(): jnp.stack([grad_piece((stack_id, 'back')) for stack_id in range(2)])]
    another operation x4 -> x2, other arithmetic: 18.7 us -> 0.81 us  [fast_body(): jnp.stack([jnp.stack([grad_piece((stack_id, layer_id)) for layer_id in ra...]
  transfers between devices with their start and end apart: 8 -> 0, of which waited for: 6 -> 0; matrix products, arithmetic and copies ran while one was open for 15% -> 0% of each run, Pallas kernels for 0% -> 0%
where the time goes in v1:
time: 686 us; the launch traced here: 678 us
  Pallas kernels  235 us (34%)
  matrix products  181 us (26%)
  local copies, waits for them, and re-layouts  170 us (25%)
  other arithmetic  83 us (12%)
  between operations  8.63 us (1%)
    pallas_call x1, Pallas kernels, reduce_grads(): pl.pallas_call(functools.partial(reduce_kernel, count), out_shape=(jax.Sh...  123 us
    pallas_call x1, Pallas kernels, gather(): pl.pallas_call(functools.partial(gather_kernel, cuts), out_shape=jax.Shap...  112 us
    concatenate x3, local copies, waits for them, and re-layouts, pack(): return jnp.concatenate(out, axis=1)  38.1 us
    unnamed x220, local copies, waits for them, and re-layouts  35.1 us
    dot_general x12, matrix products, stack_forward(): jnp.dot(inputs_kept[-1], weight, preferred_element_type=jnp.float32) + bias  32.6 us
    reduce_sum x2, other arithmetic, mean_pool(): jnp.mean(values.reshape(values.shape[0], values.shape[1] // kernel, kerne...  30.9 us
    dot_general x11, matrix products, stack_backward(): jnp.dot(d_pre, layers[layer_id][0].T, preferred_element_type=jnp.float32)  29.8 us
    reshape x2, local copies, waits for them, and re-layouts, pool_back(): return spread_out.reshape(d_pooled.shape[0], d_pooled.shape[1] * kernel)  29.5 us

profile of v1, /device:TPU:0, one launch (start us, length us, event | category | flops | bytes accessed | tf_op | source)
XLA Modules:
  0.0 678.2 jit_solution(9009277412679894471)
XLA Ops:
  4.2 5.3 reduce_sum.225
  9.5 6.2 multiply_reduce_fusion
  30.9 10.8 %subtract_divide_fusion = f32[864,3600]{1,0:T(8,128)} fusion(f32[864,3600]{1,0:T(8,128)} %param.22, f32[864]{0:T(1024)S(1)} %add_sqrt_fusion, f32[864]{0:T(1024)S(1)} %broadcast_multiply_fusion), kind=kLoop, calls=%fused_computation.8 | loop fusion | flops 6220800 | bytes 24890112 | tf_op jit(solution)/shard_map/div | solution.py:36
  41.7 14.4 %copy.50 = f32[864,3600]{0,1:T(8,128)} copy(f32[864,3600]{1,0:T(8,128)} %subtract_divide_fusion) | data formatting | bytes 24883200 | tf_op jit(solution)/shard_map/div | solution.py:36
  56.1 7.8 %bitcast_reduce_fusion = f32[864,450]{0,1:T(8,128)S(1)} fusion(f32[864,3600]{0,1:T(8,128)} %copy.50), kind=kLoop, calls=%fused_computation | loop fusion | flops 2721600 | bytes 13996800 | tf_op jit(solution)/shard_map/reduce_sum | solution.py:42
  63.9 112.2 %gather_weights.1 = bf16[8,64,18432]{2,1,0:T(8,128)(2,1)} custom-call(bf16[64,18432]{1,0:T(8,128)(2,1)} %constant_dynamic-update-slice_fusion.shard_ref), custom_call_target="tpu_custom_call" | custom-call | tf_op jit(solution)/shard_map/gather_weights/pallas_call | solution.py:401
  182.3 4.6 multiply_convert_fusion.21
  186.9 9.1 %add_subtract_fusion = f32[864,3600]{1,0:T(8,128)} fusion(f32[864,3600]{1,0:T(8,128)S(1)} %bitcast.150, bf16[864,512]{1,0:T(8,128)(2,1)S(1)} %get-tuple-element.79, f32[3600]{0:T(1024)S(1)} %get-tuple-element.78, bf16[512,18432]{1,0:T(8,128)(2,1)} %bitcast.157), kind=kOutput, calls=%fused_computation.6 | convolution fusion | flops 3191270400 | bytes 29583424 | tf_op jit(solution)/shard_map/dot_general | solution.py:100
  201.0 14.0 %copy.51 = f32[864,3600]{0,1:T(8,128)} copy(f32[864,3600]{1,0:T(8,128)} %add_subtract_fusion) | data formatting | bytes 24883200 | tf_op jit(solution)/shard_map/sub | solution.py:789
  215.0 15.1 %reshape.113 = f32[864,900,4]{0,2,1:T(4,128)} reshape(f32[864,3600]{0,1:T(8,128)} %copy.51) | data formatting | bytes 24883200 | tf_op jit(solution)/shard_map/reshape | solution.py:42
  230.1 23.1 %reduce_sum.228 = f32[864,900]{0,1:T(8,128)S(1)} reduce(f32[864,900,4]{0,2,1:T(4,128)} %reshape.113, f32[]{:T(128)} %constant.32.clone.1), dimensions={2}, to_apply=%region_3.4 | reduce | flops 2332800 | bytes 15552004 | tf_op jit(solution)/shard_map/reduce_sum | solution.py:42
  263.3 7.9 %subtract_convert_fusion = bf16[864,3600]{1,0:T(8,128)(2,1)S(1)} fusion(f32[864,3600]{1,0:T(8,128)} %add_subtract_fusion, bf16[864,512]{1,0:T(8,128)(2,1)S(1)} %get-tuple-element.81, f32[3600]{0:T(1024)S(1)} %get-tuple-element.77, bf16[512,18432]{1,0:T(8,128)(2,1)} %bitcast.163), kind=kOutput, calls=%fused_computation.5 | convolution fusion | flops 3194380800 | bytes 23749696 | tf_op jit(solution)/shard_map/dot_general | solution.py:100
  272.6 5.7 fusion.2
  287.0 7.8 %fusion.11 = f32[864,720]{0,1:T(8,128)S(1)} fusion(f32[720,720]{1,0:T(8,128)S(1)} %copy-done.13, f32[864,720]{0,1:T(8,128)S(1)} %fusion.37, f32[720]{0:T(1024)S(1)} %slice.264), kind=kOutput, calls=%fused_computation.28 | convolution fusion | flops 5375393280 | bytes 7053120 | tf_op jit(solution)/shard_map/dot_general | solution.py:96
  303.0 7.6 %convert_reduce_fusion.2 = (f32[720]{0:T(1024)S(1)}, bf16[864,720]{0,1:T(8,128)(2,1)S(1)}) fusion(f32[720,720]{1,0:T(8,128)S(1)} %copy-done.13, f32[864,720]{0,1:T(8,128)S(1)} %get-tuple-element.114, s32[864]{0:T(1024)S(1)} %copy-done.35), kind=kOutput, calls=%fused_computation.26 | convolution fusion | flops 5378503168 | bytes 5812416 | tf_op jit(solution)/shard_map/dot_general | solution.py:798
  322.7 8.0 %fusion.105 = f32[512,3600]{0,1:T(8,128)} fusion(bf16[864,512]{1,0:T(8,128)(2,1)S(1)} %get-tuple-element.88, bf16[864,3600]{1,0:T(8,128)(2,1)S(1)} %subtract_convert_fusion), kind=kOutput, calls=%fused_computation.261 | convolution fusion | flops 3185049600 | bytes 14478336 | tf_op jit(solution)/shard_map/dot_general | solution.py:124
  330.8 5.7 fusion
  336.5 9.8 %fusion.4 = f32[864,512]{1,0:T(8,128)} fusion(bf16[512,18432]{1,0:T(8,128)(2,1)} %bitcast.175, f32[864,3600]{1,0:T(8,128)S(1)} %fusion), kind=kOutput, calls=%fused_computation.17 | convolution fusion | flops 3191270400 | bytes 18012160 | tf_op jit(solution)/shard_map/dot_general | solution.py:109
  361.7 8.0 %fusion.87 = f32[512,3600]{0,1:T(8,128)} fusion(bf16[864,512]{1,0:T(8,128)(2,1)S(1)} %get-tuple-element.81, f32[864,3600]{1,0:T(8,128)S(1)} %fusion), kind=kOutput, calls=%fused_computation.249 | convolution fusion | flops 3191270400 | bytes 20699136 | tf_op jit(solution)/shard_map/dot_general | solution.py:107
  369.7 7.1 %broadcast_in_dim.4 = f32[864,900,4]{0,2,1:T(4,128)} broadcast(f32[864,900]{0,1:T(8,128)S(1)} %convolution_multiply_fusion), dimensions={0,1} | broadcast | bytes 15552000 | tf_op jit(solution)/shard_map/broadcast_in_dim | solution.py:48
  376.9 15.4 %reshape.114 = f32[864,3600]{0,1:T(8,128)} reshape(f32[864,900,4]{0,2,1:T(4,128)} %broadcast_in_dim.4) | data formatting | bytes 24883200 | tf_op jit(solution)/shard_map/reshape | solution.py:49
  392.3 14.1 %copy.52 = f32[864,3600]{1,0:T(8,128)} copy(f32[864,3600]{0,1:T(8,128)} %reshape.114) | data formatting | bytes 24883200 | tf_op jit(solution)/shard_map/reshape | solution.py:49
  406.4 9.5 %convert_reduce_fusion.1 = (f32[3600]{0:T(1024)S(1)}, bf16[864,3600]{1,0:T(8,128)(2,1)S(1)}, f32[3600]{0:T(1024)S(1)}) fusion(f32[864,3600]{1,0:T(8,128)} %copy-done, f32[864,3600]{1,0:T(8,128)} %copy.52), kind=kLoop, calls=%fused_computation.2 | loop fusion | flops 27986400 | bytes 31132800 | tf_op jit(solution)/shard_map/reduce_sum | solution.py:108
  415.9 5.8 fusion.7
  423.8 7.9 %fusion.102 = f32[512,3600]{0,1:T(8,128)} fusion(bf16[864,512]{1,0:T(8,128)(2,1)S(1)} %copy-done.11, bf16[864,3600]{1,0:T(8,128)(2,1)S(1)} %get-tuple-element.47), kind=kOutput, calls=%fused_computation.258 | convolution fusion | flops 3185049600 | bytes 14478336 | tf_op jit(solution)/shard_map/dot_general | solution.py:107
  449.7 3.9 pad_dynamic-update-slice_fusion.2
  463.6 3.9 pad_dynamic-update-slice_fusion.1
  468.2 4.3 pad_dynamic-update-slice_fusion
  480.3 36.8 %copy.53 = f32[512,18432]{1,0:T(8,128)} copy(f32[512,18432]{0,1:T(8,128)} %broadcast_dynamic-update-slice_fusion) | data formatting | bytes 75497472 | tf_op jit(solution)/shard_map/concatenate | solution.py:327
  517.1 122.7 %reduce_grads.1 = (bf16[18,2,64,512]{3,2,1,0:T(8,128)(2,1)}, f32[112,128]{1,0:T(8,128)}, f32[8,128]{1,0:T(8,128)}) custom-call(f32[4,2,64,18432]{3,2,1,0:T(8,128)} %bitcast.148, f32[112,128]{1,0:T(8,128)} %pad_bitcast_fusion.small_ref), custom_call_target="tpu_custom_call" | custom-call | tf_op jit(solution)/shard_map/reduce_grads/pallas_call | solution.py:650
  648.8 4.1 copy.54
  663.3 4.3 fusion.92
  (311 shorter events, 146.6 us)
Async XLA Ops:
  9.5 6.2 copy-start.30
  9.5 6.4 copy-start.27
  9.5 6.6 copy-start.7
  15.8 162.1 %copy-start.45 = (f32[512]{0:T(512)}, f32[512]{0:T(512)S(1)}, u32[]{:S(2)}) copy-start(f32[512]{0:T(512)S(1)} %get-tuple-element.76) | copy-start | bytes 6148
  15.8 164.1 %copy-start.43 = (f32[512]{0:T(512)}, f32[512]{0:T(512)S(1)}, u32[]{:S(2)}) copy-start(f32[512]{0:T(512)S(1)} %get-tuple-element.75) | copy-start | bytes 6148
  15.8 166.4 %copy-start.41 = (f32[512]{0:T(512)}, f32[512]{0:T(512)S(1)}, u32[]{:S(2)}) copy-start(f32[512]{0:T(512)S(1)} %get-tuple-element.74) | copy-start | bytes 6148
  15.8 166.4 %copy-start.47 = (f32[512]{0:T(512)}, f32[512]{0:T(512)S(1)}, u32[]{:S(2)}) copy-start(f32[512]{0:T(512)S(1)} %get-tuple-element.73) | copy-start | bytes 6148
  15.9 239.7 %copy-start.38 = (f32[512]{0:T(512)}, f32[512]{0:T(512)S(1)}, u32[]{:S(2)}) copy-start(f32[512]{0:T(512)S(1)} %get-tuple-element.72) | copy-start | bytes 6148
  15.9 336.1 %copy-start.36 = (f32[512]{0:T(512)}, f32[512]{0:T(512)S(1)}, u32[]{:S(2)}) copy-start(f32[512]{0:T(512)S(1)} %get-tuple-element.71) | copy-start | bytes 6148
  63.9 112.2 %copy-start.1 = (f32[864,450]{0,1:T(8,128)}, f32[864,450]{0,1:T(8,128)S(1)}, u32[]{:S(2)}) copy-start(f32[864,450]{0,1:T(8,128)S(1)} %bitcast_reduce_fusion) | copy-start | bytes 4665604
  180.0 6.9 %slice-start = ((s8[12828672]{0:T(1024)(128)(4,1)}), s8[4194304]{0:T(1024)(128)(4,1)S(1)}, s32[]{:S(2)}) async-start(s8[12828672]{0:T(1024)(128)(4,1)} %bitcast.149), calls=%async_computation | async-start | bytes 8388608
  180.0 6.9 %slice-start.1 = ((s8[12828672]{0:T(1024)(128)(4,1)}), s8[4194304]{0:T(1024)(128)(4,1)S(1)}, s32[]{:S(2)}) async-start(s8[12828672]{0:T(1024)(128)(4,1)} %bitcast.149), calls=%async_computation.1 | async-start | bytes 8388608
  186.9 9.2 %copy-start.9 = (bf16[864,512]{1,0:T(8,128)(2,1)}, bf16[864,512]{1,0:T(8,128)(2,1)S(1)}, u32[]{:S(2)}) copy-start(bf16[864,512]{1,0:T(8,128)(2,1)S(1)} %get-tuple-element.79) | copy-start | bytes 2654212
  186.9 10.4 %copy-start.29 = (f32[30,720]{1,0:T(8,128)S(1)}, f32[30,720]{1,0:T(8,128)}, u32[]{:S(2)}) copy-start(f32[30,720]{1,0:T(8,128)} %constant.51.clone) | copy-start | bytes 259204
  278.3 41.9 %copy-start.55 = (f32[864,512]{1,0:T(8,128)}, f32[864,512]{1,0:T(8,128)S(1)}, u32[]{:S(2)}) copy-start(f32[864,512]{1,0:T(8,128)S(1)} %fusion.2) | copy-start | bytes 5308420
  280.4 37.4 %copy-start.53 = (f32[864,512]{1,0:T(8,128)}, f32[864,512]{1,0:T(8,128)S(1)}, u32[]{:S(2)}) copy-start(f32[864,512]{1,0:T(8,128)S(1)} %fusion.49) | copy-start | bytes 5308420
  282.4 33.1 %copy-start.51 = (f32[864,512]{1,0:T(8,128)}, f32[864,512]{1,0:T(8,128)S(1)}, u32[]{:S(2)}) copy-start(f32[864,512]{1,0:T(8,128)S(1)} %fusion.46) | copy-start | bytes 5308420
  286.9 7.9 %copy-start.12 = (f32[864,720]{0,1:T(8,128)S(1)}, f32[864,720]{0,1:T(8,128)}, u32[]{:S(2)}) copy-start(f32[864,720]{0,1:T(8,128)} %fusion.101) | copy-start | bytes 7464964
  286.9 7.9 %copy-start.32 = (f32[60,720]{1,0:T(8,128)S(1)}, f32[60,720]{1,0:T(8,128)}, u32[]{:S(2)}) copy-start(f32[60,720]{1,0:T(8,128)} %constant.52.clone) | copy-start | bytes 518404
  286.9 7.9 %copy-start.35 = (s32[864]{0:T(1024)S(1)}, s32[864]{0:T(1024)}, u32[]{:S(2)}) copy-start(s32[864]{0:T(1024)} %param.24) | copy-start | bytes 10372
  286.9 7.9 %copy-start.50 = (f32[864,720]{0,1:T(8,128)S(1)}, f32[864,720]{0,1:T(8,128)}, u32[]{:S(2)}) copy-start(f32[864,720]{0,1:T(8,128)} %param.23) | copy-start | bytes 7464964
  336.5 25.2 %copy-start = (f32[864,3600]{1,0:T(8,128)}, f32[864,3600]{1,0:T(8,128)S(1)}, u32[]{:S(2)}) copy-start(f32[864,3600]{1,0:T(8,128)S(1)} %fusion) | copy-start | bytes 37324804
  415.9 5.9 copy-start.48
  415.9 5.9 copy-start.69
  423.8 8.0 %copy-start.72 = (bf16[864,512]{1,0:T(8,128)(2,1)}, bf16[864,512]{1,0:T(8,128)(2,1)S(1)}, u32[]{:S(2)}) copy-start(bf16[864,512]{1,0:T(8,128)(2,1)S(1)} %get-tuple-element.94) | copy-start | bytes 2654212
  423.8 7.9 %copy-start.42 = (f32[512]{0:T(512)S(1)}, f32[512]{0:T(512)}, u32[]{:S(2)}) copy-start(f32[512]{0:T(512)} %copy-done.41) | copy-start | bytes 6148
  423.8 7.9 %copy-start.64 = (f32[864,512]{1,0:T(8,128)S(1)}, f32[864,512]{1,0:T(8,128)}, u32[]{:S(2)}) copy-start(f32[864,512]{1,0:T(8,128)} %copy-done.63) | copy-start | bytes 5308420
  449.7 4.6 copy-start.17
  460.7 7.5 %slice-start.11 = ((s8[7372800]{0:T(1024)(128)(4,1)}), s8[4194304]{0:T(1024)(128)(4,1)S(1)}, s32[]{:S(2)}) async-start(s8[7372800]{0:T(1024)(128)(4,1)} %bitcast.186), calls=%async_computation.11 | async-start | bytes 8388608
  517.1 130.2 %copy-start.31 = (f32[14154]{0:T(1024)S(1)}, f32[14154]{0:T(1024)}, u32[]{:S(2)}) copy-start(f32[14154]{0:T(1024)} %param.38) | copy-start | bytes 169852
  517.1 130.2 %copy-start.33 = (f32[14154]{0:T(1024)S(1)}, f32[14154]{0:T(1024)}, u32[]{:S(2)}) copy-start(f32[14154]{0:T(1024)} %param.40) | copy-start | bytes 169852
  517.1 130.2 %copy-start.34 = (f32[14154]{0:T(1024)S(1)}, f32[14154]{0:T(1024)}, u32[]{:S(2)}) copy-start(f32[14154]{0:T(1024)} %param.39) | copy-start | bytes 169852
  (71 other events, 190.2 us)
